TPU v7x, 32 devices: a whole 2x2x4 slice. The times are simulated.
32 devices in a mesh: groups: 2 (over x), lat: 16 (over z, y, core).
Axes of the slice: x: 2, y: 2, z: 4, core: 2. Of those that a mesh axis runs over, the one named last changes fastest.
Arguments:
- mesh_latent: bfloat16 [40960, 512], P(('groups', 'lat')), parts along dimension 0, may hold values from -6 to 6
- grid_latent: bfloat16 [32768, 512], P(('groups', 'lat')), parts along dimension 0, may hold values from -6 to 6
- near_senders: int32 [32, 5, 512], P(('groups', 'lat')), parts along dimension 0, may hold values from 0 to 1279
- near_receivers: int32 [32, 5, 512], P(('groups', 'lat')), parts along dimension 0, may hold values from 0 to 1279
- near_counts: int32 [32, 5], P(('groups', 'lat')), parts along dimension 0, may hold values from 0 to 512, as said below
- near_geom: bfloat16 [32, 4, 2560], P(('groups', 'lat')), parts along dimension 0, may hold values from -6 to 6
- far_senders: int32 [32, 16, 2], P(('groups', 'lat')), parts along dimension 0, may hold values from 0 to 7
- far_receivers: int32 [32, 16, 2], P(('groups', 'lat')), parts along dimension 0, may hold values from 0 to 1279
- far_counts: int32 [32, 16], P(('groups', 'lat')), parts along dimension 0, may hold values from 0 to 2, as said below
- far_geom: bfloat16 [32, 4, 32], P(('groups', 'lat')), parts along dimension 0, may hold values from -6 to 6
- dec_senders: int32 [3, 32768], P(None, ('groups', 'lat')), parts along dimension 1, may hold values from 0 to 3839, as said below
- dec_geom: bfloat16 [4, 3, 32768], P(None, None, ('groups', 'lat')), parts along dimension 2, may hold values from -6 to 6
- edge_weights: bfloat16 [2, 3, 512, 512], replicated, may hold values from -0.25 to 0.25
- node_weights: bfloat16 [2, 3, 512, 512], replicated, may hold values from -0.1875 to 0.1875
- geom_weights: bfloat16 [2, 4, 512], replicated, may hold values from -3 to 3
- biases: float32 [4, 3, 512], replicated, may hold values from -3 to 3
- gains: float32 [4, 512], replicated, may hold values from 0.25 to 1.75
Outputs:
- mesh_out: bfloat16 [40960, 512], P(('groups', 'lat')), parts along dimension 0
- grid_out: bfloat16 [32768, 512], P(('groups', 'lat')), parts along dimension 0
There are 2 independent parts, one for each index of `groups`. A program takes and returns all parts, laid end to end along the dimension named above; an argument that names none is the same for every part. Nothing has to cross between parts.
Inputs may be any that keep to these rules, and one draw needn't show every extreme that they name: `near_counts`: A block of a source band outside 0..15 holds no live slot. Otherwise the block of the band itself holds 384 to 512 live slots, a block one band away 512 // 4 to 256, a block two bands away 512 // 8 to 128; each of these most is reached by some band in every draw. `far_counts`: every receiving band has at least one block with 2 live slots. `dec_senders`: A grid node of band b names mesh node (b - 1) * 1280 + value; on band 0 values are 1280 or more, on band 16 - 1 below 2560.
All inputs are finite; a program needn't handle non-finite values.
Results may differ from a plain program's by a relative error of at most 0.006.
Values may be sent and summed in bfloat16 or wider, within the bound.
A program may use at most 128 MiB of HBM per device.

v0:
```python
import jax
import jax.numpy as jnp
from jax import lax
from jax.sharding import PartitionSpec as P

EPSILON = 1e-05


def with_halo(value, sides, width):
    for axis, dim in sides:
        size, length = (lax.axis_size(axis), value.shape[dim])
        up = [(i, (i + 1) % size) for i in range(size - 1)]
        down = [(j, i) for i, j in up]
        last = lax.slice_in_dim(value, length - width, length, axis=dim)
        leading = lax.slice_in_dim(value, 0, width, axis=dim)
        before = lax.ppermute(last, axis, up)
        after = lax.ppermute(leading, axis, down)
        value = jnp.concatenate([before, value, after], axis=dim)
    return value


def shifted(value, axis, by):
    size = lax.axis_size(axis)
    pairs = [(i, i + by) for i in range(size) if 0 <= i + by < size]
    return lax.ppermute(value, axis, pairs)


def layer_norm(values, gain, shift):
    average = jnp.mean(values, axis=-1, keepdims=True)
    centred = values - average
    variance = jnp.mean(centred * centred, axis=-1, keepdims=True)
    return centred * lax.rsqrt(variance + EPSILON) * gain + shift


def matmul(left, right):
    return jnp.dot(left, right, preferred_element_type=jnp.float32)


def embed_geometry(geometry, weights):
    return lax.dot_general(
        geometry, weights, (((0,), (0,)), ((), ())), preferred_element_type=jnp.float32
    )


def edge_message(joined, out_weight, bias, gain):
    hidden = jax.nn.silu(joined + bias[0]).astype(jnp.bfloat16)
    output = matmul(hidden, out_weight) + bias[1]
    return layer_norm(output, gain, bias[2])


def node_update(latent, summed, weights, bias, gain):
    pre_act = matmul(latent, weights[0]) + matmul(summed.astype(jnp.bfloat16), weights[1]) + bias[0]
    hidden = jax.nn.silu(pre_act).astype(jnp.bfloat16)
    output = matmul(hidden, weights[2]) + bias[1]
    return (latent.astype(jnp.float32) + layer_norm(output, gain, bias[2])).astype(jnp.bfloat16)


def local(
    mesh_latent,
    grid_latent,
    near_senders,
    near_receivers,
    near_counts,
    near_geom,
    far_senders,
    far_receivers,
    far_counts,
    far_geom,
    dec_senders,
    dec_geom,
    edge_weights,
    node_weights,
    geom_weights,
    biases,
    gains,
):
    latent_width = mesh_latent.shape[1]
    mesh_rows = mesh_latent.shape[0]
    grid_rows = grid_latent.shape[0]
    senders = near_senders[0]
    near_live = lax.broadcasted_iota(jnp.int32, senders.shape, 1) < near_counts[0][:, None]
    far_send = far_senders[0]
    far_live = lax.broadcasted_iota(jnp.int32, far_send.shape, 1) < far_counts[0][:, None]
    nearest = with_halo(mesh_latent, (("lat", 0),), mesh_rows)
    below_two = shifted(mesh_latent, "lat", 2)
    above_two = shifted(mesh_latent, "lat", -2)
    window = jnp.concatenate([below_two, nearest, above_two], axis=0)
    window_rows = senders + lax.broadcasted_iota(jnp.int32, senders.shape, 0) * mesh_rows
    near_rows = jnp.take(window, window_rows.reshape(-1), axis=0)
    fetched_rows = jnp.take(
        mesh_latent,
        lax.all_to_all(far_send, "lat", split_axis=0, concat_axis=0, tiled=True),
        axis=0,
    )
    arrived = lax.all_to_all(fetched_rows, "lat", split_axis=0, concat_axis=0, tiled=True)
    far_rows = arrived.reshape(-1, latent_width)
    sent_proj = matmul(jnp.concatenate([near_rows, far_rows], axis=0), edge_weights[0, 0])
    receivers = jnp.concatenate([near_receivers[0].reshape(-1), far_receivers[0].reshape(-1)])
    is_live = jnp.concatenate([near_live.reshape(-1), far_live.reshape(-1)])
    geometry = jnp.concatenate([near_geom[0], far_geom[0]], axis=1)
    recv_proj = matmul(mesh_latent, edge_weights[0, 1])
    joined = (
        sent_proj
        + jnp.take(recv_proj, receivers, axis=0)
        + embed_geometry(geometry, geom_weights[0])
    )
    message = edge_message(joined, edge_weights[0, 2], biases[0], gains[0]).astype(jnp.bfloat16)
    node_ids = lax.broadcasted_iota(jnp.int32, (mesh_rows, receivers.shape[0]), 0)
    selector = ((node_ids == receivers[None, :]) & is_live[None, :]).astype(jnp.bfloat16)
    summed = matmul(selector, message)
    mesh_out = node_update(mesh_latent, summed, node_weights[0], biases[1], gains[1])
    extended = with_halo(mesh_out, (("lat", 0),), mesh_rows)
    sent_dec = matmul(extended, edge_weights[1, 0])
    recv_dec = matmul(grid_latent, edge_weights[1, 1])
    sent_rows = jnp.take(sent_dec, dec_senders.reshape(-1), axis=0).reshape(
        3, grid_rows, latent_width
    )
    geom_rows = embed_geometry(dec_geom, geom_weights[1])
    joined_grid = (sent_rows + recv_dec[None] + geom_rows).reshape(3 * grid_rows, latent_width)
    grid_message = edge_message(joined_grid, edge_weights[1, 2], biases[2], gains[2])
    summed_grid = jnp.sum(grid_message.reshape(3, grid_rows, latent_width), axis=0)
    grid_out = node_update(grid_latent, summed_grid, node_weights[1], biases[3], gains[3])
    return (mesh_out, grid_out)


def solution(mesh):
    return jax.shard_map(
        local,
        mesh=mesh,
        in_specs=(
            P(("groups", "lat"), None),
            P(("groups", "lat"), None),
            P(("groups", "lat"), None, None),
            P(("groups", "lat"), None, None),
            P(("groups", "lat"), None),
            P(("groups", "lat"), None, None),
            P(("groups", "lat"), None, None),
            P(("groups", "lat"), None, None),
            P(("groups", "lat"), None),
            P(("groups", "lat"), None, None),
            P(None, ("groups", "lat")),
            P(None, None, ("groups", "lat")),
            P(),
            P(),
            P(),
            P(),
            P(),
        ),
        out_specs=(P(("groups", "lat"), None), P(("groups", "lat"), None)),
        check_vma=False,
    )
```

profile of v0, /device:TPU:1, one launch (start us, length us, event | category | flops | bytes accessed | tf_op | source)
XLA Modules:
  0.0 246.0 jit_solution(1920663182780202145)
XLA Ops:
  0.7 5.2 %collective-permute-start = (bf16[1280,512]{1,0:T(8,128)(2,1)}, bf16[1280,512]{1,0:T(8,128)(2,1)}, u32[]{:S(2)}, u32[]{:S(2)}) collective-permute-start(bf16[1280,512]{1,0:T(8,128)(2,1)} %param.17), channel_id=1, source_target_pairs={{0,2},{1,3},{2,4},{3,5},{4,6},{5,7},{6,8},{7,9},{8,10},{9,11},{10,... | collective-permute-start | bytes 3932168 | tf_op jit(solution)/shard_map/ppermute | solution.py:25
  5.8 2.9 %collective-permute-start.1 = (bf16[1280,512]{1,0:T(8,128)(2,1)}, bf16[1280,512]{1,0:T(8,128)(2,1)}, u32[]{:S(2)}, u32[]{:S(2)}) collective-permute-start(bf16[1280,512]{1,0:T(8,128)(2,1)} %param.17), channel_id=1, source_target_pairs={{0,1},{1,2},{2,3},{3,4},{4,5},{5,6},{6,7},{7,8},{8,9},{9,10},{10,1... | collective-permute-start | bytes 3932168 | tf_op jit(solution)/shard_map/ppermute | solution.py:16
  8.8 2.4 collective-permute-start.2
  11.2 1.3 collective-permute-start.3
  12.5 1.4 copy.37
  13.9 9.1 %all-to-all-start = ((s32[16,1,2]{2,1,0:T(1,128)}), s32[16,1,2]{2,1,0:T(1,128)S(1)}, u32[]{:S(2)}, u32[]{:S(2)}) async-start(s32[16,1,2]{2,1,0:T(1,128)} %copy.37), calls=%async_computation | async-start | bytes 16384 | tf_op jit(solution)/shard_map/all_to_all | solution.py:92
  23.0 0.9 fusion.87
  24.8 0.8 copy.36
  25.7 0.7 reduce
  26.5 2.4 fusion.47
  28.9 3.4 %fusion.50 = f32[1280,512]{1,0:T(8,128)} fusion(bf16[1280,512]{1,0:T(8,128)(2,1)S(1)} %copy-done.2, bf16[2,3,512,512]{3,2,1,0:T(8,128)(2,1)} %param.30), kind=kOutput, calls=%fused_computation.62 | convolution fusion | flops 671088640 | bytes 4456448 | tf_op jit(solution)/shard_map/dot_general | solution.py:36
  32.8 2.4 copy.35
  35.3 8.1 %gather_fusion.2 = f32[2592,512]{1,0:T(8,128)} fusion(f32[1280,512]{1,0:T(8,128)S(1)} %fusion.47, s32[3072]{0:T(1024)S(1)} %pad_clamp_fusion), kind=kCustom, calls=%fused_computation.2 | custom fusion | bytes 10627200 | tf_op jit(solution)/shard_map/jit(_take)/gather | solution.py:104
  43.4 46.5 %all-to-all-done = s32[16,1,2]{2,1,0:T(1,128)S(1)} async-done(((s32[16,1,2]{2,1,0:T(1,128)}), s32[16,1,2]{2,1,0:T(1,128)S(1)}, u32[]{:S(2)}, u32[]{:S(2)}) %all-to-all-start) | async-done | bytes 160 | tf_op jit(solution)/shard_map/all_to_all | solution.py:92
  90.2 2.1 gather_fusion.1
  93.2 7.1 %all-to-all-start.1 = ((bf16[16,2,512]{2,1,0:T(2,128)(2,1)}), bf16[16,2,512]{2,1,0:T(2,128)(2,1)S(1)}, u32[]{:S(2)}, u32[]{:S(2)}) async-start(bf16[16,2,512]{2,1,0:T(2,128)(2,1)} %broadcast_select_fusion.1), calls=%async_computation.1 | async-start | bytes 65536 | tf_op jit(solution)/shard_map/all_to_all | solution.py:95
  100.3 5.9 %all-to-all-done.1 = bf16[16,2,512]{2,1,0:T(2,128)(2,1)S(1)} async-done(((bf16[16,2,512]{2,1,0:T(2,128)(2,1)}), bf16[16,2,512]{2,1,0:T(2,128)(2,1)S(1)}, u32[]{:S(2)}, u32[]{:S(2)}) %all-to-all-start.1) | async-done | bytes 32800 | tf_op jit(solution)/shard_map/all_to_all | solution.py:95
  106.3 2.5 %constant_dynamic-update-slice_fusion.5 = bf16[6400,512]{1,0:T(8,128)(2,1)} fusion(bf16[1280,512]{1,0:T(8,128)(2,1)} %collective-permute-done), kind=kLoop, calls=%fused_computation.95 | loop fusion | bytes 2621440
  108.7 2.5 %constant_dynamic-update-slice_fusion.4 = bf16[6400,512]{1,0:T(8,128)(2,1)} fusion(bf16[6400,512]{1,0:T(8,128)(2,1)} %constant_dynamic-update-slice_fusion.5, bf16[1280,512]{1,0:T(8,128)(2,1)} %collective-permute-done.1), kind=kLoop, calls=%fused_computation.94 | loop fusion | bytes 2621440
  111.2 1.2 constant_dynamic-update-slice_fusion.3
  112.4 2.5 %constant_dynamic-update-slice_fusion.2 = bf16[6400,512]{1,0:T(8,128)(2,1)} fusion(bf16[6400,512]{1,0:T(8,128)(2,1)} %constant_dynamic-update-slice_fusion.3, bf16[1280,512]{1,0:T(8,128)(2,1)} %collective-permute-done.2), kind=kLoop, calls=%fused_computation.92 | loop fusion | bytes 2621440
  114.9 2.5 %constant_dynamic-update-slice_fusion.1 = bf16[6400,512]{1,0:T(8,128)(2,1)} fusion(bf16[6400,512]{1,0:T(8,128)(2,1)} %constant_dynamic-update-slice_fusion.2, bf16[1280,512]{1,0:T(8,128)(2,1)} %collective-permute-done.3), kind=kLoop, calls=%fused_computation.91 | loop fusion | bytes 2621440 | tf_op jit(solution)/shard_map/concatenate | solution.py:87
  117.4 11.4 %gather_fusion = bf16[2560,512]{1,0:T(8,128)(2,1)S(1)} fusion(bf16[6400,512]{1,0:T(8,128)(2,1)} %constant_dynamic-update-slice_fusion.1, s32[3072]{0:T(1024)S(1)} %pad_clamp_fusion.1), kind=kCustom, calls=%fused_computation | custom fusion | bytes 5253120 | tf_op jit(solution)/shard_map/jit(_take)/gather | solution.py:89
  128.8 1.5 broadcast_select_fusion
  130.4 4.9 %fusion.15 = f32[2592,512]{1,0:T(8,128)} fusion(bf16[32,512]{1,0:T(8,128)(2,1)S(1)} %reshape.328, bf16[2560,512]{1,0:T(8,128)(2,1)S(1)} %broadcast_select_fusion, bf16[2,3,512,512]{3,2,1,0:T(8,128)(2,1)} %param.29), kind=kOutput, calls=%fused_computation.27 | convolution fusion | flops 1364262912 | bytes 8486912 | tf_op jit(solution)/shard_map/dot_general | solution.py:36
  135.4 9.6 %fusion.89 = (f32[2592]{0:T(1024)S(1)}, f32[2592,512]{1,0:T(8,128)}) fusion(f32[512]{0:T(512)S(1)} %bitcast.133, bf16[2,3,512,512]{3,2,1,0:T(8,128)(2,1)} %param.29, f32[2592,512]{1,0:T(8,128)} %fusion.15, f32[2592,512]{1,0:T(8,128)} %gather_fusion.2, f32[512]{0:T(512)S(1)} %bitcast.134, pred[2592]{0:T(1024)(128)(4,1)S(1)} %compare_and_fusion.1, ...), kind=kOutput, calls=%fused_computation.131 | convolution fusion | flops 1384208384 | bytes 16492672 | tf_op jit(solution)/shard_map/dot_general | solution.py:36
  145.0 3.6 %multiply_reduce_fusion.1 = f32[2592]{0:T(1024)S(1)} fusion(f32[2592,512]{1,0:T(8,128)} %get-tuple-element.25, f32[2592]{0:T(1024)S(1)} %broadcast_multiply_fusion.1), kind=kLoop, calls=%fused_computation.14 | loop fusion | flops 3978720 | bytes 5329152 | tf_op jit(solution)/shard_map/reduce_sum | solution.py:31
  148.6 9.1 %multiply_convert_fusion.2 = bf16[1280,512]{1,0:T(8,128)(2,1)} fusion(f32[1280,512]{1,0:T(8,128)S(1)} %copy-done.7, s32[2592]{0:T(1024)S(1)} %constant_dynamic-update-slice_fusion.6, pred[2592]{0:T(1024)(128)(4,1)S(1)} %pad_add_fusion, f32[2592,512]{1,0:T(8,128)} %get-tuple-element.25, f32[512]{0:T(512)S(1)} %bitcast.132, f32[512]{0:T(512)S(1)} %bitcast.135, ...), kind=kOutput, calls=%fused_computation.37 | convolution fusion | flops 4086988800 | bytes 9804704 | tf_op jit(solution)/shard_map/dot_general | solution.py:36
  157.7 2.5 fusion.94
  160.5 1.9 add_convert_fusion.4
  162.4 2.7 %collective-permute-start.4 = (bf16[1280,512]{0,1:T(8,128)(2,1)}, bf16[1280,512]{0,1:T(8,128)(2,1)}, u32[]{:S(2)}, u32[]{:S(2)}) collective-permute-start(bf16[1280,512]{0,1:T(8,128)(2,1)} %add_convert_fusion.4), channel_id=1, source_target_pairs={{0,1},{1,2},{2,3},{3,4},{4,5},{5,6},{6,7},{7,8},{8,9},{9,10},{10,1... | collective-permute-start | bytes 3932168 | tf_op jit(solution)/shard_map/ppermute | solution.py:16
  165.1 2.7 %collective-permute-start.5 = (bf16[1280,512]{0,1:T(8,128)(2,1)}, bf16[1280,512]{0,1:T(8,128)(2,1)}, u32[]{:S(2)}, u32[]{:S(2)}) collective-permute-start(bf16[1280,512]{0,1:T(8,128)(2,1)} %add_convert_fusion.4), channel_id=1, source_target_pairs={{1,0},{2,1},{3,2},{4,3},{5,4},{6,5},{7,6},{8,7},{9,8},{10,9},{11,1... | collective-permute-start | bytes 3932168 | tf_op jit(solution)/shard_map/ppermute | solution.py:17
  167.8 1.3 copy.43
  169.1 1.7 fusion.39
  170.9 3.1 %fusion.42 = f32[1024,512]{1,0:T(8,128)} fusion(bf16[1024,512]{1,0:T(8,128)(2,1)S(1)} %copy-done.4, bf16[2,3,512,512]{3,2,1,0:T(8,128)(2,1)} %param.30), kind=kOutput, calls=%fused_computation.54 | convolution fusion | flops 536870912 | bytes 3670016 | tf_op jit(solution)/shard_map/dot_general | solution.py:36
  174.0 3.7 %fusion.73 = f32[3,1024,512]{2,1,0:T(8,128)} fusion(bf16[4,3,1024]{2,0,1:T(4,128)(2,1)S(1)} %copy-done, bf16[2,4,512]{2,1,0:T(4,128)(2,1)S(1)} %copy-done.12), kind=kOutput, calls=%fused_computation.111 | convolution fusion | flops 12582912 | bytes 6320128 | tf_op jit(solution)/shard_map/dot_general | solution.py:40
  177.7 2.4 copy.44
  180.1 13.8 %collective-permute-done.4 = bf16[1280,512]{0,1:T(8,128)(2,1)} collective-permute-done((bf16[1280,512]{0,1:T(8,128)(2,1)}, bf16[1280,512]{0,1:T(8,128)(2,1)}, u32[]{:S(2)}, u32[]{:S(2)}) %collective-permute-start.4) | collective-permute-done | bytes 1310752 | tf_op jit(solution)/shard_map/ppermute | solution.py:16
  194.0 7.5 %fusion.5 = f32[3840,512]{1,0:T(8,128)} fusion(bf16[1280,512]{0,1:T(8,128)(2,1)} %collective-permute-done.5, bf16[1280,512]{0,1:T(8,128)(2,1)} %add_convert_fusion.4, bf16[1280,512]{0,1:T(8,128)(2,1)} %collective-permute-done.4, bf16[2,3,512,512]{3,2,1,0:T(8,128)(2,1)} %param.29), kind=kOutput, calls=%fused_computation.17 | convolution fusion | flops 2025062400 | bytes 12320768 | tf_op jit(solution)/shard_map/dot_general | solution.py:36
  201.5 17.0 %gather_fusion.3 = f32[3072,512]{1,0:T(8,128)} fusion(f32[3840,512]{1,0:T(8,128)} %fusion.5, s32[3072]{0:T(1024)S(1)} %broadcast_clamp_fusion), kind=kCustom, calls=%fused_computation.3 | custom fusion | bytes 12595200 | tf_op jit(solution)/shard_map/jit(_take)/gather | solution.py:115
  218.5 5.8 %multiply_convert_fusion = bf16[3,1024,512]{2,1,0:T(8,128)(2,1)S(1)} fusion(f32[3,1024,512]{2,1,0:T(8,128)} %fusion.73, f32[3,1024,512]{2,1,0:T(8,128)} %bitcast.108, f32[512]{0:T(512)S(1)} %bitcast.128, f32[1024,512]{1,0:T(8,128)S(1)} %fusion.39, pred[3,1024]{1,0:T(4,128)(4,1)S(1)} %compare_and_fusion), kind=kLoop, calls=%fused_computation.11 | loop fusion | flops 14155776 | bytes 17830912 | tf_op jit(solution)/shard_map/convert_element_type | solution.py:46
  224.3 3.0 %add_reduce_fusion = (f32[3072]{0:T(1024)S(1)}, f32[3072,512]{1,0:T(8,128)S(1)}) fusion(f32[512]{0:T(512)S(1)} %bitcast.119, bf16[3072,512]{1,0:T(8,128)(2,1)S(1)} %bitcast.109, bf16[2,3,512,512]{3,2,1,0:T(8,128)(2,1)} %param.29), kind=kOutput, calls=%fused_computation.12 | convolution fusion | flops 1613755392 | bytes 9975808 | tf_op jit(solution)/shard_map/dot_general | solution.py:36
  227.3 2.1 multiply_reduce_fusion
  229.4 3.6 %multiply_add_fusion = f32[3072,512]{1,0:T(8,128)} fusion(f32[3072,512]{1,0:T(8,128)S(1)} %get-tuple-element.29, f32[512]{0:T(512)S(1)} %bitcast.126, f32[512]{0:T(512)S(1)} %bitcast.127, f32[3072]{0:T(1024)S(1)} %add_rsqrt_fusion, f32[3072]{0:T(1024)S(1)} %broadcast_multiply_fusion, f32[512]{0:T(512)S(1)} %bitcast.121), kind=kLoop, calls=%fused_computation.9 | loop fusion | flops 7864320 | bytes 12613632 | tf_op jit(solution)/shard_map/add | solution.py:32
  233.0 4.9 %reduce_sum.87 = bf16[1024,512]{1,0:T(8,128)(2,1)} reduce(f32[3,1024,512]{2,1,0:T(8,128)} %bitcast.107, f32[]{:T(128)} %constant.82.clone.1), dimensions={0}, to_apply=%region_6.7 | reduce | flops 1048576 | bytes 7340036 | tf_op jit(solution)/shard_map/reduce_sum | solution.py:121
  237.9 3.8 %add_reduce_fusion.1 = (f32[1024]{0:T(1024)S(1)}, f32[1024,512]{0,1:T(8,128)S(1)}) fusion(f32[512]{0:T(512)S(1)} %bitcast.116, bf16[2,3,512,512]{3,2,1,0:T(8,128)(2,1)} %param.30, f32[1024,512]{1,0:T(8,128)} %fusion.42, f32[512]{0:T(512)S(1)} %bitcast.129, bf16[1024,512]{1,0:T(8,128)(2,1)} %reduce_sum.87), kind=kOutput, calls=%fused_computation.42 | convolution fusion | flops 1078459392 | bytes 6299648 | tf_op jit(solution)/shard_map/dot_general | solution.py:36
  242.1 1.6 add_convert_fusion.7
  243.7 2.3 copy.45
  (88 shorter events, 3.5 us)
Async XLA Ops:
  0.6 173.3 %copy-start = (bf16[4,3,1024]{2,0,1:T(4,128)(2,1)S(1)}, bf16[4,3,1024]{2,0,1:T(4,128)(2,1)}, u32[]{:S(2)}) copy-start(bf16[4,3,1024]{2,0,1:T(4,128)(2,1)} %param.28) | copy-start | bytes 73732
  0.6 28.2 %copy-start.11 = (f32[4,512]{1,0:T(4,128)S(1)}, f32[4,512]{1,0:T(4,128)}, u32[]{:S(2)}) copy-start(f32[4,512]{1,0:T(4,128)} %param.33) | copy-start | bytes 24580
  0.7 105.6 %collective-permute-start = (bf16[1280,512]{1,0:T(8,128)(2,1)}, bf16[1280,512]{1,0:T(8,128)(2,1)}, u32[]{:S(2)}, u32[]{:S(2)}) collective-permute-start(bf16[1280,512]{1,0:T(8,128)(2,1)} %param.17), channel_id=1, source_target_pairs={{0,2},{1,3},{2,4},{3,5},{4,6},{5,7},{6,8},{7,9},{8,10},{9,11},{10,... | collective-permute-start | bytes 3932168 | tf_op jit(solution)/shard_map/ppermute | solution.py:25
  5.8 102.9 %collective-permute-start.1 = (bf16[1280,512]{1,0:T(8,128)(2,1)}, bf16[1280,512]{1,0:T(8,128)(2,1)}, u32[]{:S(2)}, u32[]{:S(2)}) collective-permute-start(bf16[1280,512]{1,0:T(8,128)(2,1)} %param.17), channel_id=1, source_target_pairs={{0,1},{1,2},{2,3},{3,4},{4,5},{5,6},{6,7},{7,8},{8,9},{9,10},{10,1... | collective-permute-start | bytes 3932168 | tf_op jit(solution)/shard_map/ppermute | solution.py:16
  8.8 103.6 %collective-permute-start.2 = (bf16[1280,512]{1,0:T(8,128)(2,1)}, bf16[1280,512]{1,0:T(8,128)(2,1)}, u32[]{:S(2)}, u32[]{:S(2)}) collective-permute-start(bf16[1280,512]{1,0:T(8,128)(2,1)} %param.17), channel_id=1, source_target_pairs={{1,0},{2,1},{3,2},{4,3},{5,4},{6,5},{7,6},{8,7},{9,8},{10,9},{11,1... | collective-permute-start | bytes 3932168 | tf_op jit(solution)/shard_map/ppermute | solution.py:17
  11.2 103.7 %collective-permute-start.3 = (bf16[1280,512]{1,0:T(8,128)(2,1)}, bf16[1280,512]{1,0:T(8,128)(2,1)}, u32[]{:S(2)}, u32[]{:S(2)}) collective-permute-start(bf16[1280,512]{1,0:T(8,128)(2,1)} %param.17), channel_id=1, source_target_pairs={{2,0},{3,1},{4,2},{5,3},{6,4},{7,5},{8,6},{9,7},{10,8},{11,9},{12,... | collective-permute-start | bytes 3932168 | tf_op jit(solution)/shard_map/ppermute | solution.py:25
  13.9 76.0 %all-to-all-start = ((s32[16,1,2]{2,1,0:T(1,128)}), s32[16,1,2]{2,1,0:T(1,128)S(1)}, u32[]{:S(2)}, u32[]{:S(2)}) async-start(s32[16,1,2]{2,1,0:T(1,128)} %copy.37), calls=%async_computation | async-start | bytes 16384 | tf_op jit(solution)/shard_map/all_to_all | solution.py:92
  26.4 2.5 %copy-start.2 = (bf16[1280,512]{1,0:T(8,128)(2,1)S(1)}, bf16[1280,512]{1,0:T(8,128)(2,1)}, u32[]{:S(2)}) copy-start(bf16[1280,512]{1,0:T(8,128)(2,1)} %param.17) | copy-start | bytes 3932164
  28.8 3.5 %copy-start.13 = (s32[1,5]{1,0:T(1,128)S(1)}, s32[1,5]{1,0:T(1,128)}, u32[]{:S(2)}) copy-start(s32[1,5]{1,0:T(1,128)} %param.21) | copy-start | bytes 64
  28.9 3.5 %copy-start.8 = (s32[3,1024]{1,0:T(4,128)S(1)}, s32[3,1024]{1,0:T(4,128)}, u32[]{:S(2)}) copy-start(s32[3,1024]{1,0:T(4,128)} %param.27) | copy-start | bytes 36868
  28.9 3.6 %copy-start.9 = (s32[1,5,512]{2,0,1:T(1,128)S(1)}, s32[1,5,512]{2,0,1:T(1,128)}, u32[]{:S(2)}) copy-start(s32[1,5,512]{2,0,1:T(1,128)} %param.19) | copy-start | bytes 30724
  28.9 3.6 %copy-start.14 = (s32[1,16]{1,0:T(1,128)S(1)}, s32[1,16]{1,0:T(1,128)}, u32[]{:S(2)}) copy-start(s32[1,16]{1,0:T(1,128)} %param.25) | copy-start | bytes 196
  28.9 3.8 %copy-start.10 = (s32[1,5,512]{2,0,1:T(1,128)S(1)}, s32[1,5,512]{2,0,1:T(1,128)}, u32[]{:S(2)}) copy-start(s32[1,5,512]{2,0,1:T(1,128)} %param.20) | copy-start | bytes 30724
  43.4 67.8 %copy-start.3 = (bf16[1280,512]{1,0:T(8,128)(2,1)S(1)}, bf16[1280,512]{1,0:T(8,128)(2,1)}, u32[]{:S(2)}) copy-start(bf16[1280,512]{1,0:T(8,128)(2,1)} %param.17) | copy-start | bytes 3932164
  93.2 13.1 %all-to-all-start.1 = ((bf16[16,2,512]{2,1,0:T(2,128)(2,1)}), bf16[16,2,512]{2,1,0:T(2,128)(2,1)S(1)}, u32[]{:S(2)}, u32[]{:S(2)}) async-start(bf16[16,2,512]{2,1,0:T(2,128)(2,1)} %broadcast_select_fusion.1), calls=%async_computation.1 | async-start | bytes 65536 | tf_op jit(solution)/shard_map/all_to_all | solution.py:95
  130.4 5.0 %copy-start.12 = (bf16[2,4,512]{2,1,0:T(4,128)(2,1)S(1)}, bf16[2,4,512]{2,1,0:T(4,128)(2,1)}, u32[]{:S(2)}) copy-start(bf16[2,4,512]{2,1,0:T(4,128)(2,1)} %param.31) | copy-start | bytes 24580
  130.4 5.0 %copy-start.15 = (bf16[1,4,2560]{2,1,0:T(4,128)(2,1)S(1)}, bf16[1,4,2560]{2,1,0:T(4,128)(2,1)}, u32[]{:S(2)}) copy-start(bf16[1,4,2560]{2,1,0:T(4,128)(2,1)} %param.22) | copy-start | bytes 61444
  130.4 5.0 %copy-start.16 = (bf16[1,4,32]{2,1,0:T(4,128)(2,1)S(1)}, bf16[1,4,32]{2,1,0:T(4,128)(2,1)}, u32[]{:S(2)}) copy-start(bf16[1,4,32]{2,1,0:T(4,128)(2,1)} %param.26) | copy-start | bytes 772
  145.0 3.6 %copy-start.7 = (f32[1280,512]{1,0:T(8,128)S(1)}, f32[1280,512]{1,0:T(8,128)}, u32[]{:S(2)}) copy-start(f32[1280,512]{1,0:T(8,128)} %fusion.50) | copy-start | bytes 7864324
  157.7 2.8 %copy-start.5 = (bf16[1280,512]{0,1:T(8,128)(2,1)S(1)}, bf16[1280,512]{0,1:T(8,128)(2,1)}, u32[]{:S(2)}) copy-start(bf16[1280,512]{0,1:T(8,128)(2,1)} %copy.35) | copy-start | bytes 3932164
  160.5 7.3 %copy-start.4 = (bf16[1024,512]{1,0:T(8,128)(2,1)S(1)}, bf16[1024,512]{1,0:T(8,128)(2,1)}, u32[]{:S(2)}) copy-start(bf16[1024,512]{1,0:T(8,128)(2,1)} %param.18) | copy-start | bytes 3145732
  162.4 31.6 %collective-permute-start.4 = (bf16[1280,512]{0,1:T(8,128)(2,1)}, bf16[1280,512]{0,1:T(8,128)(2,1)}, u32[]{:S(2)}, u32[]{:S(2)}) collective-permute-start(bf16[1280,512]{0,1:T(8,128)(2,1)} %add_convert_fusion.4), channel_id=1, source_target_pairs={{0,1},{1,2},{2,3},{3,4},{4,5},{5,6},{6,7},{7,8},{8,9},{9,10},{10,1... | collective-permute-start | bytes 3932168 | tf_op jit(solution)/shard_map/ppermute | solution.py:16
  165.1 28.9 %collective-permute-start.5 = (bf16[1280,512]{0,1:T(8,128)(2,1)}, bf16[1280,512]{0,1:T(8,128)(2,1)}, u32[]{:S(2)}, u32[]{:S(2)}) collective-permute-start(bf16[1280,512]{0,1:T(8,128)(2,1)} %add_convert_fusion.4), channel_id=1, source_target_pairs={{1,0},{2,1},{3,2},{4,3},{5,4},{6,5},{7,6},{8,7},{9,8},{10,9},{11,1... | collective-permute-start | bytes 3932168 | tf_op jit(solution)/shard_map/ppermute | solution.py:17
  237.9 4.2 %copy-start.6 = (bf16[1024,512]{0,1:T(8,128)(2,1)S(1)}, bf16[1024,512]{0,1:T(8,128)(2,1)}, u32[]{:S(2)}) copy-start(bf16[1024,512]{0,1:T(8,128)(2,1)} %copy.43) | copy-start | bytes 3145732
  242.0 3.9 %copy-start.1 = (bf16[4,3,1024]{2,0,1:T(4,128)(2,1)S(1)}, bf16[4,3,1024]{2,0,1:T(4,128)(2,1)}, u32[]{:S(2)}) copy-start(bf16[4,3,1024]{2,0,1:T(4,128)(2,1)} %param.28) | copy-start | bytes 73732
where the time goes:
time: 248 us; the launch traced here: 246 us
  waiting for transfers between devices  66.3 us (27%)
  local copies, waits for them, and re-layouts  62.2 us (25%)
  matrix products  54.7 us (22%)
  starting transfers between devices  33.4 us (13%)
  other arithmetic  28.2 us (11%)
    dot_general x11, matrix products, matmul(): return jnp.dot(left, right, preferred_element_type=jnp.float32)  51 us
    all_to_all x1, waiting for transfers between devices, local(): lax.all_to_all(far_send, 'lat', split_axis=0, concat_axis=0, tiled=True)  46.5 us
    unnamed x47, local copies, waits for them, and re-layouts  18 us
    gather x1, local copies, waits for them, and re-layouts, local(): jnp.take(sent_dec, dec_senders.reshape(-1), axis=0)  17 us
    ppermute x2, waiting for transfers between devices, with_halo(): before = lax.ppermute(last, axis, up)  13.9 us
    gather x1, local copies, waits for them, and re-layouts, local(): near_rows = jnp.take(window, window_rows.reshape(-1), axis=0)  11.4 us
    all_to_all x1, starting transfers between devices, local(): lax.all_to_all(far_send, 'lat', split_axis=0, concat_axis=0, tiled=True)  9.07 us
    gather x1, local copies, waits for them, and re-layouts, local(): jnp.take(recv_proj, receivers, axis=0)  8.1 us
  transfers between devices with their start and end apart: 8, of which 3 were waited for; matrix products, arithmetic and copies ran while one was open for 19% of the time, Pallas kernels for 0%

commit v1 on v0

v1 whole, which is shorter than its diff:
```python
import functools

import jax
import jax.numpy as jnp
from jax import lax
from jax.experimental import pallas as pl
from jax.experimental.pallas import tpu as pltpu
from jax.sharding import PartitionSpec as P

EPSILON = 1e-05
MESH = pl.DeviceIdType.MESH
F32 = jnp.float32
BF16 = jnp.bfloat16
CHUNK = 256
HOT_ROWS = 16


def dot(left, right):
    return jnp.dot(left, right, preferred_element_type=F32)


def silu(value):
    half = 0.5 * value
    return half + half * jnp.tanh(half)


def layer_norm(values, gain, shift):
    average = jnp.mean(values, axis=-1, keepdims=True)
    centred = values - average
    variance = jnp.mean(centred * centred, axis=-1, keepdims=True)
    return centred * lax.rsqrt(variance + EPSILON) * gain + shift


def one_hot(column, first, count):
    ids = lax.broadcasted_iota(jnp.int32, (column.shape[0], count), 1) + first
    return jnp.where(ids == column, 1.0, 0.0).astype(BF16)


def kernel(
    n, caps,
    latent, near_send, idx_rows, geo_rows, dec_rows, dec_geo, geom_w, biases, gains,
    grid_hbm, ew_hbm, nw_hbm,
    mesh_hbm, grid_out_hbm,
    ew, nw, grid, idx_in, served, sent, hot, cols, geo_cols, dec_cols, dec_geo_cols,
    pre_edge, msg, pre_node, mout, win, acc, pre_grid, pre_gnode, gout,
    load_sem, idx_send, idx_recv, row_send, row_recv, hot_send, hot_recv,
    halo_send, halo_recv, out_sem, gout_sem,
):
    me = lax.axis_index("lat")
    rows = latent.shape[0]
    grid_rows = grid.shape[0]
    edges = idx_rows.shape[1]
    near_edges = sum(cap for _, cap in caps)
    own = caps[0][1]
    far_edges = edges - near_edges

    def peer(by):
        return {"lat": lax.rem(me + by + 2 * n, n)}

    loads = [
        pltpu.make_async_copy(ew_hbm, ew, load_sem.at[0]),
        pltpu.make_async_copy(nw_hbm, nw, load_sem.at[1]),
        pltpu.make_async_copy(grid_hbm, grid, load_sem.at[2]),
    ]
    for load in loads:
        load.start()

    barrier = pltpu.get_barrier_semaphore()

    @pl.loop(1, n)
    def _(k):
        pl.semaphore_signal(barrier, inc=1, device_id=peer(k), device_id_type=MESH)

    pl.semaphore_wait(barrier, n - 1)

    requests = []
    starts, at = ({}, 0)
    for j, cap in caps:
        starts[j] = at
        at += cap
    for slot, (j, cap) in enumerate(caps[1:]):
        requests.append(pltpu.make_async_remote_copy(
            src_ref=near_send, dst_ref=idx_in.at[slot],
            send_sem=idx_send.at[slot], recv_sem=idx_recv.at[slot],
            device_id=peer(j - 2), device_id_type=MESH,
        ))
        requests[-1].start()

    def hot_copy(k):
        return pltpu.make_async_remote_copy(
            src_ref=latent.at[pl.ds(0, HOT_ROWS)],
            dst_ref=hot.at[pl.ds(pl.multiple_of(me * HOT_ROWS, HOT_ROWS), HOT_ROWS)],
            send_sem=hot_send.at[k], recv_sem=hot_recv.at[k],
            device_id=peer(k), device_id_type=MESH,
        )

    @pl.loop(1, n)
    def _(k):
        hot_copy(k).start()

    hot[pl.ds(pl.multiple_of(me * HOT_ROWS, HOT_ROWS), HOT_ROWS), :] = latent[0:HOT_ROWS, :]

    cols[...] = jnp.transpose(idx_rows[...])
    geo_cols[...] = jnp.transpose(geo_rows[...])

    replies = []
    for slot, (j, cap) in enumerate(caps[1:]):
        requests[slot].wait_recv()
        wanted = jnp.transpose(jnp.broadcast_to(idx_in[slot, j:j + 1, :cap], (8, cap)))
        place = starts[j] - own
        served[place:place + cap, :] = dot(
            one_hot(wanted[:, 0:1], 0, rows), latent[...]).astype(BF16)
        replies.append(pltpu.make_async_remote_copy(
            src_ref=served.at[pl.ds(place, cap)],
            dst_ref=sent.at[pl.ds(place, cap)],
            send_sem=row_send.at[slot], recv_sem=row_recv.at[slot],
            device_id=peer(2 - j), device_id_type=MESH,
        ))
        replies[-1].start()

    loads[0].wait()
    loads[1].wait()

    def received(start, count):
        here = pl.ds(start, count)
        picked = dot(one_hot(cols[here, 0:1], 0, rows), latent[...]).astype(BF16)
        pre_edge[here, :] = (
            dot(picked, ew[0, 1])
            + dot(geo_cols[here, :].astype(BF16), geom_w[0])
            + biases[0, 0:1, :]
        )

    def message(sent_rows, start, count):
        here = pl.ds(start, count)
        hidden = silu(dot(sent_rows, ew[0, 0]) + pre_edge[here, :]).astype(BF16)
        output = dot(hidden, ew[0, 2]) + biases[0, 1:2, :]
        msg[here, :] = layer_norm(output, gains[0:1, :], biases[0, 2:3, :]).astype(BF16)

    @pl.loop(0, near_edges // CHUNK)
    def _(c):
        received(pl.multiple_of(c * CHUNK, CHUNK), CHUNK)

    received(near_edges, far_edges)

    @pl.loop(0, own // CHUNK)
    def _(c):
        start = pl.multiple_of(c * CHUNK, CHUNK)
        picked = dot(one_hot(cols[pl.ds(start, CHUNK), 1:2], 0, rows), latent[...])
        message(picked.astype(BF16), start, CHUNK)

    @pl.loop(0, rows // CHUNK)
    def _(c):
        here = pl.ds(pl.multiple_of(c * CHUNK, CHUNK), CHUNK)
        pre_node[here, :] = dot(latent[here, :], nw[0, 0]) + biases[1, 0:1, :]

    @pl.loop(1, n)
    def _(k):
        hot_copy(k).wait_recv()

    hot_rows = dot(one_hot(cols[near_edges:edges, 1:2], 0, n * HOT_ROWS), hot[...])
    message(hot_rows.astype(BF16), near_edges, far_edges)

    for reply in replies:
        reply.wait_recv()

    @pl.loop(0, (near_edges - own) // CHUNK)
    def _(c):
        start = pl.multiple_of(c * CHUNK, CHUNK)
        message(sent[pl.ds(start, CHUNK), :], pl.multiple_of(own + start, CHUNK), CHUNK)

    def halo_copy(side, c):
        here = pl.ds(pl.multiple_of(c * CHUNK, CHUNK), CHUNK)
        return pltpu.make_async_remote_copy(
            src_ref=mout.at[here], dst_ref=win.at[side, here],
            send_sem=halo_send.at[side, c], recv_sem=halo_recv.at[side, c],
            device_id=peer(1 - 2 * side), device_id_type=MESH,
        )

    @pl.loop(0, rows // CHUNK)
    def _(c):
        first = pl.multiple_of(c * CHUNK, CHUNK)
        here = pl.ds(first, CHUNK)
        ids = lax.broadcasted_iota(jnp.int32, (CHUNK, edges), 0) + first
        selector = jnp.where(ids == idx_rows[2:3, :], 1.0, 0.0).astype(BF16)
        summed = dot(selector, msg[...]).astype(BF16)
        hidden = silu(pre_node[here, :] + dot(summed, nw[0, 1])).astype(BF16)
        output = dot(hidden, nw[0, 2]) + biases[1, 1:2, :]
        updated = layer_norm(output, gains[1:2, :], biases[1, 2:3, :])
        mout[here, :] = (latent[here, :].astype(F32) + updated).astype(BF16)
        halo_copy(0, c).start()
        halo_copy(1, c).start()

    store_mesh = pltpu.make_async_copy(mout, mesh_hbm, out_sem)
    store_mesh.start()

    dec_cols[...] = jnp.transpose(dec_rows[...])
    for k in range(3):
        dec_geo_cols[k] = jnp.transpose(dec_geo[k])
    loads[2].wait()

    @pl.loop(0, grid_rows // CHUNK)
    def _(c):
        here = pl.ds(pl.multiple_of(c * CHUNK, CHUNK), CHUNK)
        latents = grid[here, :]
        pre_grid[here, :] = dot(latents, ew[1, 1]) + biases[2, 0:1, :]
        pre_gnode[here, :] = dot(latents, nw[1, 0]) + biases[3, 0:1, :]
        for k in range(3):
            acc[k, here, :] = dot(
                one_hot(dec_cols[here, k:k + 1], rows, rows), mout[...]).astype(BF16)

    chunks = rows // CHUNK
    early = (chunks + 1) // 2 * CHUNK

    def neighbours(column, first, count):
        return (
            dot(one_hot(column, first, count), win[0, first:first + count, :])
            + dot(one_hot(column, 2 * rows + first, count), win[1, first:first + count, :])
        )

    for c in range(early // CHUNK):
        halo_copy(0, c).wait_recv()
        halo_copy(1, c).wait_recv()

    @pl.loop(0, grid_rows // CHUNK)
    def _(c):
        here = pl.ds(pl.multiple_of(c * CHUNK, CHUNK), CHUNK)
        for k in range(3):
            acc[k, here, :] = (
                acc[k, here, :].astype(F32) + neighbours(dec_cols[here, k:k + 1], 0, early)
            ).astype(BF16)

    for c in range(early // CHUNK, chunks):
        halo_copy(0, c).wait_recv()
        halo_copy(1, c).wait_recv()

    def store_grid(c):
        here = pl.ds(pl.multiple_of(c * CHUNK, CHUNK), CHUNK)
        return pltpu.make_async_copy(gout.at[here], grid_out_hbm.at[here], gout_sem.at[c])

    @pl.loop(0, grid_rows // CHUNK)
    def _(c):
        here = pl.ds(pl.multiple_of(c * CHUNK, CHUNK), CHUNK)
        total = jnp.zeros((CHUNK, latent.shape[1]), F32)
        for k in range(3):
            picked = (
                acc[k, here, :].astype(F32)
                + neighbours(dec_cols[here, k:k + 1], early, rows - early)
            ).astype(BF16)
            pre = (
                dot(picked, ew[1, 0]) + pre_grid[here, :]
                + dot(dec_geo_cols[k, here, :].astype(BF16), geom_w[1])
            )
            output = dot(silu(pre).astype(BF16), ew[1, 2]) + biases[2, 1:2, :]
            total += layer_norm(output, gains[2:3, :], biases[2, 2:3, :])
        hidden = silu(pre_gnode[here, :] + dot(total.astype(BF16), nw[1, 1])).astype(BF16)
        output = dot(hidden, nw[1, 2]) + biases[3, 1:2, :]
        updated = layer_norm(output, gains[3:4, :], biases[3, 2:3, :])
        gout[here, :] = (grid[here, :].astype(F32) + updated).astype(BF16)
        store_grid(c).start()

    for c in range(grid_rows // CHUNK):
        store_grid(c).wait()
    store_mesh.wait()
    for request in requests:
        request.wait_send()
    for reply in replies:
        reply.wait_send()

    @pl.loop(1, n)
    def _(k):
        hot_copy(k).wait_send()

    for c in range(chunks):
        halo_copy(0, c).wait_send()
        halo_copy(1, c).wait_send()


def pad_rows(value, count):
    return jnp.pad(value, ((0, count - value.shape[0]),) + ((0, 0),) * (value.ndim - 1))


def local(
    mesh_latent, grid_latent, near_senders, near_receivers, near_counts, near_geom,
    far_senders, far_receivers, far_counts, far_geom, dec_senders, dec_geom,
    edge_weights, node_weights, geom_weights, biases, gains,
):
    n = lax.axis_size("lat")
    rows, width = mesh_latent.shape
    grid_rows = grid_latent.shape[0]
    cap = near_senders.shape[2]
    caps = ((2, cap), (1, cap // 2), (3, cap // 2), (0, cap // 4), (4, cap // 4))
    far_slots = far_senders.shape[1] * far_senders.shape[2]
    far_padded = -(-far_slots // 128) * 128

    def joined(near, far, fill=0):
        far = jnp.pad(far.reshape(-1), (0, far_padded - far_slots), constant_values=fill)
        return jnp.concatenate([near[j, :c] for j, c in caps] + [far])

    near_live = lax.broadcasted_iota(jnp.int32, near_senders.shape[1:], 1) < near_counts[0][:, None]
    far_live = lax.broadcasted_iota(jnp.int32, far_senders.shape[1:], 1) < far_counts[0][:, None]
    hot_index = far_senders[0] + HOT_ROWS * lax.broadcasted_iota(jnp.int32, far_senders.shape[1:], 0)
    idx_rows = pad_rows(jnp.stack([
        joined(near_receivers[0], far_receivers[0]),
        joined(near_senders[0], hot_index),
        joined(
            jnp.where(near_live, near_receivers[0], -1),
            jnp.where(far_live, far_receivers[0], -1), -1,
        ),
    ]), 8)
    near_geo = near_geom[0].reshape(4, 5, cap)
    geo_rows = pad_rows(jnp.concatenate(
        [near_geo[:, j, :c] for j, c in caps]
        + [jnp.pad(far_geom[0], ((0, 0), (0, far_padded - far_slots)))], axis=1,
    ).astype(F32), 8)
    edges = idx_rows.shape[1]
    remote = sum(c for _, c in caps[1:])
    dec_rows = pad_rows(dec_senders, 8)
    dec_geo = jnp.pad(dec_geom.transpose(1, 0, 2).astype(F32), ((0, 0), (0, 4), (0, 0)))
    geom_w = jnp.pad(geom_weights, ((0, 0), (0, 4), (0, 0)))
    chunks = rows // CHUNK

    vmem = pl.BlockSpec(memory_space=pltpu.VMEM)
    hbm = pl.BlockSpec(memory_space=pl.ANY)
    dma = pltpu.SemaphoreType.DMA
    return pl.pallas_call(
        functools.partial(kernel, n, caps),
        out_shape=(
            jax.ShapeDtypeStruct((rows, width), BF16),
            jax.ShapeDtypeStruct((grid_rows, width), BF16),
        ),
        in_specs=[vmem] * 9 + [hbm] * 3,
        out_specs=(hbm, hbm),
        scratch_shapes=[
            pltpu.VMEM(edge_weights.shape, BF16),
            pltpu.VMEM(node_weights.shape, BF16),
            pltpu.VMEM((grid_rows, width), BF16),
            pltpu.VMEM((4, 5, cap), jnp.int32),
            pltpu.VMEM((remote, width), BF16),
            pltpu.VMEM((remote, width), BF16),
            pltpu.VMEM((n * HOT_ROWS, width), BF16),
            pltpu.VMEM((edges, 8), jnp.int32),
            pltpu.VMEM((edges, 8), F32),
            pltpu.VMEM((grid_rows, 8), jnp.int32),
            pltpu.VMEM((3, grid_rows, 8), F32),
            pltpu.VMEM((edges, width), F32),
            pltpu.VMEM((edges, width), BF16),
            pltpu.VMEM((rows, width), F32),
            pltpu.VMEM((rows, width), BF16),
            pltpu.VMEM((2, rows, width), BF16),
            pltpu.VMEM((3, grid_rows, width), BF16),
            pltpu.VMEM((grid_rows, width), F32),
            pltpu.VMEM((grid_rows, width), F32),
            pltpu.VMEM((grid_rows, width), BF16),
            dma((3,)), dma((4,)), dma((4,)), dma((4,)), dma((4,)), dma((n,)), dma((n,)),
            dma((2, chunks)), dma((2, chunks)), dma, dma((grid_rows // CHUNK,)),
        ],
        compiler_params=pltpu.CompilerParams(
            collective_id=0, has_side_effects=True, vmem_limit_bytes=56 * 2**20,
        ),
        cost_estimate=pl.CostEstimate(flops=40_000_000_000, bytes_accessed=16_000_000, transcendentals=4_000_000),
    )(
        mesh_latent, near_senders[0], idx_rows, geo_rows, dec_rows, dec_geo, geom_w, biases, gains,
        grid_latent, edge_weights, node_weights,
    )


def solution(mesh):
    return jax.shard_map(
        local,
        mesh=mesh,
        in_specs=(
            P(("groups", "lat"), None),
            P(("groups", "lat"), None),
            P(("groups", "lat"), None, None),
            P(("groups", "lat"), None, None),
            P(("groups", "lat"), None),
            P(("groups", "lat"), None, None),
            P(("groups", "lat"), None, None),
            P(("groups", "lat"), None, None),
            P(("groups", "lat"), None),
            P(("groups", "lat"), None, None),
            P(None, ("groups", "lat")),
            P(None, None, ("groups", "lat")),
            P(),
            P(),
            P(),
            P(),
            P(),
        ),
        out_specs=(P(("groups", "lat"), None), P(("groups", "lat"), None)),
        check_vma=False,
    )
```

time: 248 us -> 95.3 us (0.38)
  Pallas kernels: 0 us -> 72.9 us
  waiting for transfers between devices: 66.3 us -> 0 us
  matrix products: 54.7 us -> 0 us
  local copies, waits for them, and re-layouts: 62.2 us -> 17.2 us
  starting transfers between devices: 33.4 us -> 0 us
  other arithmetic: 28.2 us -> 3.56 us
    pallas_call x0 -> x1, Pallas kernels: none -> 72.9 us  [local(): pl.pallas_call(functools.partial(kernel, n, caps), out_shape=(jax.ShapeDt...]
    dot_general x12 -> x0, matrix products: 54.7 us -> none  [the longest x11 51 us: matmul(): return jnp.dot(left, right, preferred_element_type=jnp.float32)]
    all_to_all x2 -> x0, waiting for transfers between devices: 52.4 us -> none  [the longest x1 46.5 us: local(): lax.all_to_all(far_send, 'lat', split_axis=0, concat_axis=0, tiled=True)]
    gather x5 -> x0, local copies, waits for them, and re-layouts: 38.7 us -> none  [the longest x1 17 us: local(): jnp.take(sent_dec, dec_senders.reshape(-1), axis=0)]
    ppermute x6 -> x0, starting transfers between devices: 17.2 us -> none  [the longest x2 6.47 us: shifted(): return lax.ppermute(value, axis, pairs)]
    all_to_all x2 -> x0, starting transfers between devices: 16.2 us -> none  [the longest x1 9.07 us: local(): lax.all_to_all(far_send, 'lat', split_axis=0, concat_axis=0, tiled=True)]
    ppermute x6 -> x0, waiting for transfers between devices: 13.9 us -> none  [the longest x2 13.9 us: with_halo(): before = lax.ppermute(last, axis, up)]
    reduce_sum x5 -> x0, other arithmetic: 11.2 us -> none  [the longest x4 6.36 us: layer_norm(): variance = jnp.mean(centred * centred, axis=-1, keepdims=True)]
  transfers between devices with their start and end apart: 8 -> 0, of which waited for: 3 -> 0; matrix products, arithmetic and copies ran while one was open for 19% -> 0% of each run, Pallas kernels for 0% -> 0%
where the time goes in v1:
time: 95.3 us; the launch traced here: 94.5 us
  Pallas kernels  72.9 us (76%)
  local copies, waits for them, and re-layouts  17.2 us (18%)
  other arithmetic  3.56 us (4%)
    pallas_call x1, Pallas kernels, local(): pl.pallas_call(functools.partial(kernel, n, caps), out_shape=(jax.ShapeDt...  72.9 us
    unnamed x31, local copies, waits for them, and re-layouts  11.4 us
    pad x2, local copies, waits for them, and re-layouts, pad_rows(): jnp.pad(value, ((0, count - value.shape[0]),) + ((0, 0),) * (value.ndim -...  1.95 us

profile of v1, /device:TPU:1, one launch (start us, length us, event | category | flops | bytes accessed | tf_op | source)
XLA Modules:
  0.0 94.5 jit_solution(15658499593892480018)
XLA Ops:
  0.6 0.7 iota_compare_fusion.1
  1.4 0.1 lt.30
  1.5 0.7 slice.67
  2.2 0.7 slice.62
  2.8 0.1 iota.21
  2.9 0.1 iota.22
  3.0 0.8 copy.23
  3.8 0.1 squeeze.87
  3.9 0.8 copy.22
  4.6 0.1 reshape_squeeze.6
  4.8 0.7 constant_dynamic-update-slice_fusion.8
  5.5 0.7 constant_dynamic-update-slice_fusion.7
  6.2 0.7 constant_dynamic-update-slice_fusion.6
  6.8 0.7 constant_dynamic-update-slice_fusion.5
  7.5 0.7 constant_dynamic-update-slice_fusion.4
  8.2 0.7 constant_dynamic-update-slice_fusion.3
  8.9 0.8 fusion
  9.8 1.3 %pad.48.geom_w = bf16[2,8,512]{2,1,0:T(8,128)(2,1)} pad(bf16[2,4,512]{2,1,0:T(4,128)(2,1)} %param.31, bf16[]{:T(256)} %constant.9.clone.1), padding=0_0x0_4x0_0 | pad | bytes 24578 | tf_op jit(solution)/shard_map/jit(_pad)/pad | solution.py:319
  11.1 0.7 copy.32
  11.8 0.0 copy-start.1
  11.9 0.7 copy.31
  12.7 0.6 pad.41.idx_rows
  13.3 1.3 %pad.45.dec_rows = s32[8,1024]{1,0:T(8,128)} pad(s32[3,1024]{1,0:T(4,128)} %param.27, s32[]{:T(128)} %constant.6.clone.1), padding=0_5x0_0 | pad | bytes 45060 | tf_op jit(solution)/shard_map/jit(_pad)/pad | solution.py:279
  14.7 1.4 %copy.24.biases = f32[4,3,512]{2,1,0:T(4,128)} copy(f32[4,3,512]{2,0,1:T(4,128)} %param.32) | data formatting | bytes 49152 | tf_op args[15]
  16.0 0.6 pad_convert_fusion.1.geo_rows
  16.7 1.4 %pad_convert_fusion.dec_geo = f32[3,8,1024]{2,1,0:T(8,128)} fusion(bf16[3,4,1024]{2,1,0:T(4,128)(2,1)} %bitcast.66), kind=kLoop, calls=%fused_computation | loop fusion | flops 24576 | bytes 122880 | tf_op jit(solution)/shard_map/jit(_pad)/pad | solution.py:318
  18.0 0.0 copy-done.1
  18.0 72.9 %shard_map.176 = (bf16[1280,512]{1,0:T(8,128)(2,1)}, bf16[1024,512]{1,0:T(8,128)(2,1)}) custom-call(bf16[1280,512]{1,0:T(8,128)(2,1)} %latent.1, s32[5,512]{1,0:T(8,128)} %bitcast.70, s32[8,1408]{1,0:T(8,128)} %pad.41.idx_rows, f32[8,1408]{1,0:T(8,128)} %pad_convert_fusion.1.geo_rows, s32[8,1024]{1,0:T(8,128)} %pad.45.dec_rows, ...), custom_call_target="tpu_custom_call" | custom-call | flops 40000000000 | bytes 16000000 | tf_op jit(solution)/shard_map/pallas_call | solution.py:325
  91.0 0.0 copy-start
  91.0 2.5 %copy.58 = bf16[1280,512]{1,0:T(8,128)(2,1)} copy(bf16[1280,512]{1,0:T(8,128)(2,1)} %get-tuple-element.10) | data formatting | bytes 2621440
  93.5 0.0 copy-done
  93.5 1.0 %copy.59 = bf16[1024,512]{1,0:T(8,128)(2,1)} copy(bf16[1024,512]{1,0:T(8,128)(2,1)S(1)} %copy-done) | data formatting | bytes 2097152
  (32 shorter events, 0.2 us)
Async XLA Ops:
  11.8 6.2 %copy-start.1 = (s32[1,5,512]{2,1,0:T(8,128)}, s32[1,5,512]{2,1,0:T(8,128)S(1)}, u32[]{:S(2)}) copy-start(s32[1,5,512]{2,1,0:T(8,128)S(1)} %copy.32) | copy-start | bytes 30724
  91.0 2.6 %copy-start = (bf16[1024,512]{1,0:T(8,128)(2,1)S(1)}, bf16[1024,512]{1,0:T(8,128)(2,1)}, u32[]{:S(2)}) copy-start(bf16[1024,512]{1,0:T(8,128)(2,1)} %get-tuple-element.11) | copy-start | bytes 3145732

commit v2 on v1

--- a/solution.py
+++ b/solution.py
@@ -37,10 +37,14 @@
 
 
 def kernel(
-    n, caps,
-    latent, near_send, idx_rows, geo_rows, dec_rows, dec_geo, geom_w, biases, gains,
-    grid_hbm, ew_hbm, nw_hbm,
+    n, caps, far_cap,
+    latent_hbm, grid_hbm, send_hbm, recv_hbm, counts_hbm, geom_hbm,
+    far_send_hbm, far_recv_hbm, far_counts_hbm, far_geom_hbm,
+    dec_send_hbm, dec_geom_hbm, ew_hbm, nw_hbm, geom_w_hbm, biases_hbm, gains_hbm,
     mesh_hbm, grid_out_hbm,
+    latent, near_recv, near_send, counts, near_geom, far_send, far_recv, far_counts, far_geom,
+    dec_send, dec_geom, geom_raw, biases, gains,
+    idx_rows, geo_rows, dec_rows, dec_geo_rows, geom_w,
     ew, nw, grid, idx_in, served, sent, hot, cols, geo_cols, dec_cols, dec_geo_cols,
     pre_edge, msg, pre_node, mout, win, acc, pre_grid, pre_gnode, gout,
     load_sem, idx_send, idx_recv, row_send, row_recv, hot_send, hot_recv,
@@ -57,30 +61,43 @@
     def peer(by):
         return {"lat": lax.rem(me + by + 2 * n, n)}
 
+    barrier = pltpu.get_barrier_semaphore()
+
+    @pl.loop(1, n)
+    def _(k):
+        pl.semaphore_signal(barrier, inc=1, device_id=peer(k), device_id_type=MESH)
+
+    pairs = (
+        (latent_hbm, latent), (send_hbm, near_send), (recv_hbm, near_recv), (counts_hbm, counts),
+        (geom_hbm, near_geom), (far_send_hbm, far_send), (far_recv_hbm, far_recv),
+        (far_counts_hbm, far_counts), (far_geom_hbm, far_geom), (dec_send_hbm, dec_send),
+        (dec_geom_hbm, dec_geom), (geom_w_hbm, geom_raw), (biases_hbm, biases), (gains_hbm, gains),
+        (ew_hbm, ew), (nw_hbm, nw), (grid_hbm, grid),
+    )
     loads = [
-        pltpu.make_async_copy(ew_hbm, ew, load_sem.at[0]),
-        pltpu.make_async_copy(nw_hbm, nw, load_sem.at[1]),
-        pltpu.make_async_copy(grid_hbm, grid, load_sem.at[2]),
+        pltpu.make_async_copy(source, target, load_sem.at[i])
+        for i, (source, target) in enumerate(pairs)
     ]
     for load in loads:
         load.start()
 
-    barrier = pltpu.get_barrier_semaphore()
-
-    @pl.loop(1, n)
-    def _(k):
-        pl.semaphore_signal(barrier, inc=1, device_id=peer(k), device_id_type=MESH)
-
-    pl.semaphore_wait(barrier, n - 1)
-
-    requests = []
     starts, at = ({}, 0)
     for j, cap in caps:
         starts[j] = at
         at += cap
+    idx_rows[...] = jnp.zeros_like(idx_rows)
+    idx_rows[2:3, :] = jnp.full((1, edges), -1, jnp.int32)
+    geo_rows[...] = jnp.zeros_like(geo_rows)
+    dec_rows[...] = jnp.zeros_like(dec_rows)
+    dec_geo_rows[...] = jnp.zeros_like(dec_geo_rows)
+    geom_w[...] = jnp.zeros_like(geom_w)
+
+    pl.semaphore_wait(barrier, n - 1)
+
+    requests = []
     for slot, (j, cap) in enumerate(caps[1:]):
         requests.append(pltpu.make_async_remote_copy(
-            src_ref=near_send, dst_ref=idx_in.at[slot],
+            src_ref=send_hbm, dst_ref=idx_in.at[slot],
             send_sem=idx_send.at[slot], recv_sem=idx_recv.at[slot],
             device_id=peer(j - 2), device_id_type=MESH,
         ))
@@ -88,7 +105,7 @@
 
     def hot_copy(k):
         return pltpu.make_async_remote_copy(
-            src_ref=latent.at[pl.ds(0, HOT_ROWS)],
+            src_ref=latent_hbm.at[pl.ds(0, HOT_ROWS)],
             dst_ref=hot.at[pl.ds(pl.multiple_of(me * HOT_ROWS, HOT_ROWS), HOT_ROWS)],
             send_sem=hot_send.at[k], recv_sem=hot_recv.at[k],
             device_id=peer(k), device_id_type=MESH,
@@ -98,15 +115,39 @@
     def _(k):
         hot_copy(k).start()
 
+    for load in loads[:14]:
+        load.wait()
     hot[pl.ds(pl.multiple_of(me * HOT_ROWS, HOT_ROWS), HOT_ROWS), :] = latent[0:HOT_ROWS, :]
 
+    for j, cap in caps:
+        here = slice(starts[j], starts[j] + cap)
+        to = near_recv[j, :, :cap]
+        live = lax.broadcasted_iota(jnp.int32, (1, cap), 1) < counts[0:1, j:j + 1]
+        idx_rows[0:1, here] = to
+        idx_rows[1:2, here] = near_send[j, :, :cap]
+        idx_rows[2:3, here] = jnp.where(live, to, -1)
+        first = j * near_recv.shape[2]
+        geo_rows[0:4, here] = near_geom[:, first:first + cap].astype(F32)
+    wide = far_edges // far_cap
+    for c in range(far_cap):
+        first = near_edges + c * wide
+        here = slice(first, first + n)
+        to = far_recv[c:c + 1, :]
+        idx_rows[0:1, here] = to
+        idx_rows[1:2, here] = far_send[c:c + 1, :] + HOT_ROWS * lax.broadcasted_iota(jnp.int32, (1, n), 1)
+        idx_rows[2:3, here] = jnp.where(far_counts[0:1, :] > c, to, -1)
+        place = lax.broadcasted_iota(jnp.int32, (far_cap * n, wide), 0)
+        slots = far_cap * lax.broadcasted_iota(jnp.int32, (far_cap * n, wide), 1) + c
+        geo_rows[0:4, first:first + wide] = dot(
+            far_geom[...], jnp.where(place == slots, 1.0, 0.0).astype(BF16))
+    geom_w[:, 0:4, :] = geom_raw[...].astype(F32)
     cols[...] = jnp.transpose(idx_rows[...])
     geo_cols[...] = jnp.transpose(geo_rows[...])
 
     replies = []
     for slot, (j, cap) in enumerate(caps[1:]):
         requests[slot].wait_recv()
-        wanted = jnp.transpose(jnp.broadcast_to(idx_in[slot, j:j + 1, :cap], (8, cap)))
+        wanted = jnp.transpose(jnp.broadcast_to(idx_in[slot, j, :, :cap], (8, cap)))
         place = starts[j] - own
         served[place:place + cap, :] = dot(
             one_hot(wanted[:, 0:1], 0, rows), latent[...]).astype(BF16)
@@ -118,23 +159,23 @@
         ))
         replies[-1].start()
 
-    loads[0].wait()
-    loads[1].wait()
+    loads[14].wait()
+    loads[15].wait()
 
     def received(start, count):
         here = pl.ds(start, count)
         picked = dot(one_hot(cols[here, 0:1], 0, rows), latent[...]).astype(BF16)
         pre_edge[here, :] = (
             dot(picked, ew[0, 1])
-            + dot(geo_cols[here, :].astype(BF16), geom_w[0])
+            + dot(geo_cols[here, :].astype(BF16), geom_w[0].astype(BF16))
             + biases[0, 0:1, :]
         )
 
     def message(sent_rows, start, count):
         here = pl.ds(start, count)
         hidden = silu(dot(sent_rows, ew[0, 0]) + pre_edge[here, :]).astype(BF16)
-        output = dot(hidden, ew[0, 2]) + biases[0, 1:2, :]
-        msg[here, :] = layer_norm(output, gains[0:1, :], biases[0, 2:3, :]).astype(BF16)
+        output = dot(hidden, ew[0, 2]) + biases[1, 0:1, :]
+        msg[here, :] = layer_norm(output, gains[0:1, :], biases[2, 0:1, :]).astype(BF16)
 
     @pl.loop(0, near_edges // CHUNK)
     def _(c):
@@ -151,7 +192,7 @@
     @pl.loop(0, rows // CHUNK)
     def _(c):
         here = pl.ds(pl.multiple_of(c * CHUNK, CHUNK), CHUNK)
-        pre_node[here, :] = dot(latent[here, :], nw[0, 0]) + biases[1, 0:1, :]
+        pre_node[here, :] = dot(latent[here, :], nw[0, 0]) + biases[0, 1:2, :]
 
     @pl.loop(1, n)
     def _(k):
@@ -185,7 +226,7 @@
         summed = dot(selector, msg[...]).astype(BF16)
         hidden = silu(pre_node[here, :] + dot(summed, nw[0, 1])).astype(BF16)
         output = dot(hidden, nw[0, 2]) + biases[1, 1:2, :]
-        updated = layer_norm(output, gains[1:2, :], biases[1, 2:3, :])
+        updated = layer_norm(output, gains[1:2, :], biases[2, 1:2, :])
         mout[here, :] = (latent[here, :].astype(F32) + updated).astype(BF16)
         halo_copy(0, c).start()
         halo_copy(1, c).start()
@@ -193,23 +234,25 @@
     store_mesh = pltpu.make_async_copy(mout, mesh_hbm, out_sem)
     store_mesh.start()
 
+    dec_rows[0:3, :] = dec_send[...]
     dec_cols[...] = jnp.transpose(dec_rows[...])
     for k in range(3):
-        dec_geo_cols[k] = jnp.transpose(dec_geo[k])
-    loads[2].wait()
+        dec_geo_rows[0:4, :] = dec_geom[k].astype(F32)
+        dec_geo_cols[k] = jnp.transpose(dec_geo_rows[...])
+    loads[16].wait()
 
     @pl.loop(0, grid_rows // CHUNK)
     def _(c):
         here = pl.ds(pl.multiple_of(c * CHUNK, CHUNK), CHUNK)
         latents = grid[here, :]
-        pre_grid[here, :] = dot(latents, ew[1, 1]) + biases[2, 0:1, :]
-        pre_gnode[here, :] = dot(latents, nw[1, 0]) + biases[3, 0:1, :]
+        pre_grid[here, :] = dot(latents, ew[1, 1]) + biases[0, 2:3, :]
+        pre_gnode[here, :] = dot(latents, nw[1, 0]) + biases[0, 3:4, :]
         for k in range(3):
             acc[k, here, :] = dot(
                 one_hot(dec_cols[here, k:k + 1], rows, rows), mout[...]).astype(BF16)
 
     chunks = rows // CHUNK
-    early = (chunks + 1) // 2 * CHUNK
+    early = (chunks - 1) * CHUNK
 
     def neighbours(column, first, count):
         return (
@@ -248,13 +291,13 @@
             ).astype(BF16)
             pre = (
                 dot(picked, ew[1, 0]) + pre_grid[here, :]
-                + dot(dec_geo_cols[k, here, :].astype(BF16), geom_w[1])
+                + dot(dec_geo_cols[k, here, :].astype(BF16), geom_w[1].astype(BF16))
             )
-            output = dot(silu(pre).astype(BF16), ew[1, 2]) + biases[2, 1:2, :]
+            output = dot(silu(pre).astype(BF16), ew[1, 2]) + biases[1, 2:3, :]
             total += layer_norm(output, gains[2:3, :], biases[2, 2:3, :])
         hidden = silu(pre_gnode[here, :] + dot(total.astype(BF16), nw[1, 1])).astype(BF16)
-        output = dot(hidden, nw[1, 2]) + biases[3, 1:2, :]
-        updated = layer_norm(output, gains[3:4, :], biases[3, 2:3, :])
+        output = dot(hidden, nw[1, 2]) + biases[1, 3:4, :]
+        updated = layer_norm(output, gains[3:4, :], biases[2, 3:4, :])
         gout[here, :] = (grid[here, :].astype(F32) + updated).astype(BF16)
         store_grid(c).start()
 
@@ -273,10 +316,6 @@
     for c in range(chunks):
         halo_copy(0, c).wait_send()
         halo_copy(1, c).wait_send()
-
-
-def pad_rows(value, count):
-    return jnp.pad(value, ((0, count - value.shape[0]),) + ((0, 0),) * (value.ndim - 1))
 
 
 def local(
@@ -288,53 +327,41 @@
     rows, width = mesh_latent.shape
     grid_rows = grid_latent.shape[0]
     cap = near_senders.shape[2]
+    far_cap = far_senders.shape[2]
     caps = ((2, cap), (1, cap // 2), (3, cap // 2), (0, cap // 4), (4, cap // 4))
-    far_slots = far_senders.shape[1] * far_senders.shape[2]
-    far_padded = -(-far_slots // 128) * 128
-
-    def joined(near, far, fill=0):
-        far = jnp.pad(far.reshape(-1), (0, far_padded - far_slots), constant_values=fill)
-        return jnp.concatenate([near[j, :c] for j, c in caps] + [far])
-
-    near_live = lax.broadcasted_iota(jnp.int32, near_senders.shape[1:], 1) < near_counts[0][:, None]
-    far_live = lax.broadcasted_iota(jnp.int32, far_senders.shape[1:], 1) < far_counts[0][:, None]
-    hot_index = far_senders[0] + HOT_ROWS * lax.broadcasted_iota(jnp.int32, far_senders.shape[1:], 0)
-    idx_rows = pad_rows(jnp.stack([
-        joined(near_receivers[0], far_receivers[0]),
-        joined(near_senders[0], hot_index),
-        joined(
-            jnp.where(near_live, near_receivers[0], -1),
-            jnp.where(far_live, far_receivers[0], -1), -1,
-        ),
-    ]), 8)
-    near_geo = near_geom[0].reshape(4, 5, cap)
-    geo_rows = pad_rows(jnp.concatenate(
-        [near_geo[:, j, :c] for j, c in caps]
-        + [jnp.pad(far_geom[0], ((0, 0), (0, far_padded - far_slots)))], axis=1,
-    ).astype(F32), 8)
-    edges = idx_rows.shape[1]
+    edges = sum(c for _, c in caps) + far_cap * (-(-n // 128) * 128)
     remote = sum(c for _, c in caps[1:])
-    dec_rows = pad_rows(dec_senders, 8)
-    dec_geo = jnp.pad(dec_geom.transpose(1, 0, 2).astype(F32), ((0, 0), (0, 4), (0, 0)))
-    geom_w = jnp.pad(geom_weights, ((0, 0), (0, 4), (0, 0)))
     chunks = rows // CHUNK
-
-    vmem = pl.BlockSpec(memory_space=pltpu.VMEM)
+    operands = (
+        mesh_latent, grid_latent, near_senders.transpose(1, 0, 2), near_receivers.transpose(1, 0, 2),
+        near_counts, near_geom[0], far_senders.transpose(0, 2, 1)[0], far_receivers.transpose(0, 2, 1)[0],
+        far_counts, far_geom[0], dec_senders, dec_geom.transpose(1, 0, 2),
+        edge_weights, node_weights, geom_weights, biases.transpose(1, 0, 2), gains,
+    )
+
+    def like(i):
+        return pltpu.VMEM(operands[i].shape, operands[i].dtype)
+
     hbm = pl.BlockSpec(memory_space=pl.ANY)
     dma = pltpu.SemaphoreType.DMA
     return pl.pallas_call(
-        functools.partial(kernel, n, caps),
+        functools.partial(kernel, n, caps, far_cap),
         out_shape=(
             jax.ShapeDtypeStruct((rows, width), BF16),
             jax.ShapeDtypeStruct((grid_rows, width), BF16),
         ),
-        in_specs=[vmem] * 9 + [hbm] * 3,
+        in_specs=[hbm] * len(operands),
         out_specs=(hbm, hbm),
         scratch_shapes=[
-            pltpu.VMEM(edge_weights.shape, BF16),
-            pltpu.VMEM(node_weights.shape, BF16),
-            pltpu.VMEM((grid_rows, width), BF16),
-            pltpu.VMEM((4, 5, cap), jnp.int32),
+            like(0), like(3), like(2), like(4), like(5), like(6), like(7), like(8), like(9),
+            like(10), like(11), like(14), like(15), like(16),
+            pltpu.VMEM((8, edges), jnp.int32),
+            pltpu.VMEM((8, edges), F32),
+            pltpu.VMEM((8, grid_rows), jnp.int32),
+            pltpu.VMEM((8, grid_rows), F32),
+            pltpu.VMEM((2, 8, width), F32),
+            like(12), like(13), like(1),
+            pltpu.VMEM((4, 5, 1, cap), jnp.int32),
             pltpu.VMEM((remote, width), BF16),
             pltpu.VMEM((remote, width), BF16),
             pltpu.VMEM((n * HOT_ROWS, width), BF16),
@@ -351,17 +378,15 @@
             pltpu.VMEM((grid_rows, width), F32),
             pltpu.VMEM((grid_rows, width), F32),
             pltpu.VMEM((grid_rows, width), BF16),
-            dma((3,)), dma((4,)), dma((4,)), dma((4,)), dma((4,)), dma((n,)), dma((n,)),
+            dma((len(operands),)), dma((4,)), dma((4,)), dma((4,)), dma((4,)), dma((n,)), dma((n,)),
             dma((2, chunks)), dma((2, chunks)), dma, dma((grid_rows // CHUNK,)),
         ],
         compiler_params=pltpu.CompilerParams(
-            collective_id=0, has_side_effects=True, vmem_limit_bytes=56 * 2**20,
+            collective_id=0, has_side_effects=True, vmem_limit_bytes=58 * 2**20,
         ),
-        cost_estimate=pl.CostEstimate(flops=40_000_000_000, bytes_accessed=16_000_000, transcendentals=4_000_000),
-    )(
-        mesh_latent, near_senders[0], idx_rows, geo_rows, dec_rows, dec_geo, geom_w, biases, gains,
-        grid_latent, edge_weights, node_weights,
-    )
+        cost_estimate=pl.CostEstimate(
+            flops=25_000_000_000, bytes_accessed=12_000_000, transcendentals=4_000_000),
+    )(*operands)
 
 
 def solution(mesh):

time: 95.3 us -> 79.5 us (0.83)
  local copies, waits for them, and re-layouts: 17.2 us -> 3.52 us
  other arithmetic: 3.56 us -> 0 us
  Pallas kernels: 72.9 us -> 75.2 us
    unnamed x31 -> x4, local copies, waits for them, and re-layouts: 11.4 us -> 3.52 us
    pad x3 -> x0, local copies, waits for them, and re-layouts: 3.26 us -> none  [the longest x2 1.95 us: pad_rows(): jnp.pad(value, ((0, count - value.shape[0]),) + ((0, 0),) * (value.ndim -...]
    pallas_call x1, Pallas kernels: 72.9 us -> 75.2 us  [local(): pl.pallas_call(functools.partial(kernel, n, caps, far_cap), out_shape=(ja...]
    pad x2 -> x0, other arithmetic: 2.01 us -> none  [the longest x1 1.39 us: local(): jnp.pad(dec_geom.transpose(1, 0, 2).astype(F32), ((0, 0), (0, 4), (0, 0)))]
    slice x6 -> x0, local copies, waits for them, and re-layouts: 1.39 us -> none  [joined(): return jnp.concatenate([near[j, :c] for j, c in caps] + [far])]
where the time goes in v2:
time: 79.5 us; the launch traced here: 79.3 us
  Pallas kernels  75.2 us (95%)
  local copies, waits for them, and re-layouts  3.52 us (4%)
    pallas_call x1, Pallas kernels, local(): pl.pallas_call(functools.partial(kernel, n, caps, far_cap), out_shape=(ja...  75.2 us
    unnamed x4, local copies, waits for them, and re-layouts  3.52 us

profile of v2, /device:TPU:1, one launch (start us, length us, event | category | flops | bytes accessed | tf_op | source)
XLA Modules:
  0.0 79.3 jit_solution(15069006560097217753)
XLA Ops:
  0.6 75.2 %shard_map.176 = (bf16[1280,512]{1,0:T(8,128)(2,1)}, bf16[1024,512]{1,0:T(8,128)(2,1)}) custom-call(bf16[1280,512]{1,0:T(8,128)(2,1)} %latent_hbm.1, bf16[1024,512]{1,0:T(8,128)(2,1)} %grid_hbm.1, s32[5,1,512]{2,1,0:T(1,128)} %bitcast.15, s32[5,1,512]{2,1,0:T(1,128)} %bitcast.16, s32[1,5]{1,0:T(1,128)} %counts_hbm.1, bf16[4,2560]{1,0:T(4,128)(2,1)} %bitcast.14, ...), custom_call_target="tpu_custom_call" | custom-call | flops 24999999488 | bytes 12000000 | tf_op jit(solution)/shard_map/pallas_call | solution.py:347
  75.8 0.0 copy-start
  75.8 2.5 %copy.21 = bf16[1280,512]{1,0:T(8,128)(2,1)} copy(bf16[1280,512]{1,0:T(8,128)(2,1)} %get-tuple-element.4) | data formatting | bytes 2621440
  78.4 0.0 copy-done
  78.4 1.0 %copy.22 = bf16[1024,512]{1,0:T(8,128)(2,1)} copy(bf16[1024,512]{1,0:T(8,128)(2,1)S(1)} %copy-done) | data formatting | bytes 2097152
Async XLA Ops:
  75.8 2.6 %copy-start = (bf16[1024,512]{1,0:T(8,128)(2,1)S(1)}, bf16[1024,512]{1,0:T(8,128)(2,1)}, u32[]{:S(2)}) copy-start(bf16[1024,512]{1,0:T(8,128)(2,1)} %get-tuple-element.5) | copy-start | bytes 3145732

commit v3 on v2

--- a/solution.py
+++ b/solution.py
@@ -85,13 +85,6 @@
     for j, cap in caps:
         starts[j] = at
         at += cap
-    idx_rows[...] = jnp.zeros_like(idx_rows)
-    idx_rows[2:3, :] = jnp.full((1, edges), -1, jnp.int32)
-    geo_rows[...] = jnp.zeros_like(geo_rows)
-    dec_rows[...] = jnp.zeros_like(dec_rows)
-    dec_geo_rows[...] = jnp.zeros_like(dec_geo_rows)
-    geom_w[...] = jnp.zeros_like(geom_w)
-
     pl.semaphore_wait(barrier, n - 1)
 
     requests = []
@@ -115,7 +108,30 @@
     def _(k):
         hot_copy(k).start()
 
-    for load in loads[:14]:
+    loads[0].wait()
+
+    replies = []
+    for slot, (j, cap) in enumerate(caps[1:]):
+        requests[slot].wait_recv()
+        wanted = jnp.transpose(jnp.broadcast_to(idx_in[slot, j, :, :cap], (8, cap)))
+        place = starts[j] - own
+        served[place:place + cap, :] = dot(
+            one_hot(wanted[:, 0:1], 0, rows), latent[...]).astype(BF16)
+        replies.append(pltpu.make_async_remote_copy(
+            src_ref=served.at[pl.ds(place, cap)],
+            dst_ref=sent.at[pl.ds(place, cap)],
+            send_sem=row_send.at[slot], recv_sem=row_recv.at[slot],
+            device_id=peer(2 - j), device_id_type=MESH,
+        ))
+        replies[-1].start()
+
+    idx_rows[...] = jnp.zeros_like(idx_rows)
+    idx_rows[2:3, :] = jnp.full((1, edges), -1, jnp.int32)
+    geo_rows[...] = jnp.zeros_like(geo_rows)
+    dec_rows[...] = jnp.zeros_like(dec_rows)
+    dec_geo_rows[...] = jnp.zeros_like(dec_geo_rows)
+    geom_w[...] = jnp.zeros_like(geom_w)
+    for load in loads[1:14]:
         load.wait()
     hot[pl.ds(pl.multiple_of(me * HOT_ROWS, HOT_ROWS), HOT_ROWS), :] = latent[0:HOT_ROWS, :]
 
@@ -144,21 +160,6 @@
     cols[...] = jnp.transpose(idx_rows[...])
     geo_cols[...] = jnp.transpose(geo_rows[...])
 
-    replies = []
-    for slot, (j, cap) in enumerate(caps[1:]):
-        requests[slot].wait_recv()
-        wanted = jnp.transpose(jnp.broadcast_to(idx_in[slot, j, :, :cap], (8, cap)))
-        place = starts[j] - own
-        served[place:place + cap, :] = dot(
-            one_hot(wanted[:, 0:1], 0, rows), latent[...]).astype(BF16)
-        replies.append(pltpu.make_async_remote_copy(
-            src_ref=served.at[pl.ds(place, cap)],
-            dst_ref=sent.at[pl.ds(place, cap)],
-            send_sem=row_send.at[slot], recv_sem=row_recv.at[slot],
-            device_id=peer(2 - j), device_id_type=MESH,
-        ))
-        replies[-1].start()
-
     loads[14].wait()
     loads[15].wait()
 
@@ -216,6 +217,9 @@
             send_sem=halo_send.at[side, c], recv_sem=halo_recv.at[side, c],
             device_id=peer(1 - 2 * side), device_id_type=MESH,
         )
+
+    quick = 1 - lax.rem(me, 2)
+    slow = 1 - quick
 
     @pl.loop(0, rows // CHUNK)
     def _(c):
@@ -228,8 +232,8 @@
         output = dot(hidden, nw[0, 2]) + biases[1, 1:2, :]
         updated = layer_norm(output, gains[1:2, :], biases[2, 1:2, :])
         mout[here, :] = (latent[here, :].astype(F32) + updated).astype(BF16)
-        halo_copy(0, c).start()
-        halo_copy(1, c).start()
+        halo_copy(quick, c).start()
+        halo_copy(slow, c).start()
 
     store_mesh = pltpu.make_async_copy(mout, mesh_hbm, out_sem)
     store_mesh.start()
@@ -247,34 +251,42 @@
         latents = grid[here, :]
         pre_grid[here, :] = dot(latents, ew[1, 1]) + biases[0, 2:3, :]
         pre_gnode[here, :] = dot(latents, nw[1, 0]) + biases[0, 3:4, :]
+
+    chunks = rows // CHUNK
+
+    def from_side(side, column, first, count):
+        offset = side * 2 * rows + first
+        return dot(one_hot(column, offset, count), win[side, first:first + count, :])
+
+    for c in range(chunks):
+        halo_copy(quick, c).wait_recv()
+
+    @pl.loop(0, grid_rows // CHUNK)
+    def _(c):
+        here = pl.ds(pl.multiple_of(c * CHUNK, CHUNK), CHUNK)
         for k in range(3):
-            acc[k, here, :] = dot(
-                one_hot(dec_cols[here, k:k + 1], rows, rows), mout[...]).astype(BF16)
-
-    chunks = rows // CHUNK
+            column = dec_cols[here, k:k + 1]
+            acc[k, here, :] = (
+                dot(one_hot(column, rows, rows), mout[...]) + from_side(quick, column, 0, rows)
+            ).astype(BF16)
+
     early = (chunks - 1) * CHUNK
-
-    def neighbours(column, first, count):
-        return (
-            dot(one_hot(column, first, count), win[0, first:first + count, :])
-            + dot(one_hot(column, 2 * rows + first, count), win[1, first:first + count, :])
-        )
-
-    for c in range(early // CHUNK):
-        halo_copy(0, c).wait_recv()
-        halo_copy(1, c).wait_recv()
-
-    @pl.loop(0, grid_rows // CHUNK)
-    def _(c):
-        here = pl.ds(pl.multiple_of(c * CHUNK, CHUNK), CHUNK)
-        for k in range(3):
-            acc[k, here, :] = (
-                acc[k, here, :].astype(F32) + neighbours(dec_cols[here, k:k + 1], 0, early)
-            ).astype(BF16)
+    middle = early // CHUNK // 2 * CHUNK
+    for first, last in ((0, middle), (middle, early)):
+        for c in range(first // CHUNK, last // CHUNK):
+            halo_copy(slow, c).wait_recv()
+
+        @pl.loop(0, grid_rows // CHUNK)
+        def _(c, first=first, last=last):
+            here = pl.ds(pl.multiple_of(c * CHUNK, CHUNK), CHUNK)
+            for k in range(3):
+                acc[k, here, :] = (
+                    acc[k, here, :].astype(F32)
+                    + from_side(slow, dec_cols[here, k:k + 1], first, last - first)
+                ).astype(BF16)
 
     for c in range(early // CHUNK, chunks):
-        halo_copy(0, c).wait_recv()
-        halo_copy(1, c).wait_recv()
+        halo_copy(slow, c).wait_recv()
 
     def store_grid(c):
         here = pl.ds(pl.multiple_of(c * CHUNK, CHUNK), CHUNK)
@@ -287,7 +299,7 @@
         for k in range(3):
             picked = (
                 acc[k, here, :].astype(F32)
-                + neighbours(dec_cols[here, k:k + 1], early, rows - early)
+                + from_side(slow, dec_cols[here, k:k + 1], early, rows - early)
             ).astype(BF16)
             pre = (
                 dot(picked, ew[1, 0]) + pre_grid[here, :]

time: 79.5 us -> 74.1 us (0.932)
  Pallas kernels: 75.2 us -> 69.8 us
    pallas_call x1, Pallas kernels: 75.2 us -> 69.8 us  [local(): pl.pallas_call(functools.partial(kernel, n, caps, far_cap), out_shape=(ja...]
where the time goes in v3:
time: 74.1 us; the launch traced here: 74 us
  Pallas kernels  69.8 us (94%)
  local copies, waits for them, and re-layouts  3.52 us (5%)
    pallas_call x1, Pallas kernels, local(): pl.pallas_call(functools.partial(kernel, n, caps, far_cap), out_shape=(ja...  69.8 us
    unnamed x4, local copies, waits for them, and re-layouts  3.52 us

profile of v3, /device:TPU:1, one launch (start us, length us, event | category | flops | bytes accessed | tf_op | source)
XLA Modules:
  0.0 74.0 jit_solution(13513994498065311660)
XLA Ops:
  0.6 69.8 %shard_map.176 = (bf16[1280,512]{1,0:T(8,128)(2,1)}, bf16[1024,512]{1,0:T(8,128)(2,1)}) custom-call(bf16[1280,512]{1,0:T(8,128)(2,1)} %latent_hbm.1, bf16[1024,512]{1,0:T(8,128)(2,1)} %grid_hbm.1, s32[5,1,512]{2,1,0:T(1,128)} %bitcast.15, s32[5,1,512]{2,1,0:T(1,128)} %bitcast.16, s32[1,5]{1,0:T(1,128)} %counts_hbm.1, bf16[4,2560]{1,0:T(4,128)(2,1)} %bitcast.14, ...), custom_call_target="tpu_custom_call" | custom-call | flops 24999999488 | bytes 12000000 | tf_op jit(solution)/shard_map/pallas_call | solution.py:359
  70.4 0.0 copy-start
  70.4 2.5 %copy.21 = bf16[1280,512]{1,0:T(8,128)(2,1)} copy(bf16[1280,512]{1,0:T(8,128)(2,1)} %get-tuple-element.4) | data formatting | bytes 2621440
  73.0 0.0 copy-done
  73.0 1.0 %copy.22 = bf16[1024,512]{1,0:T(8,128)(2,1)} copy(bf16[1024,512]{1,0:T(8,128)(2,1)S(1)} %copy-done) | data formatting | bytes 2097152
Async XLA Ops:
  70.4 2.6 %copy-start = (bf16[1024,512]{1,0:T(8,128)(2,1)S(1)}, bf16[1024,512]{1,0:T(8,128)(2,1)}, u32[]{:S(2)}) copy-start(bf16[1024,512]{1,0:T(8,128)(2,1)} %get-tuple-element.5) | copy-start | bytes 3145732
